TPU v7x, 512 devices: a whole 4x8x8 slice. The times are simulated.
512 devices in a mesh: gx: 64 (over z, y), gy: 8 (over x, core).
Axes of the slice: x: 4, y: 8, z: 8, core: 2. Of those that a mesh axis runs over, the one named last changes fastest.
Arguments:
- forward_coeff: float32 [192, 65536], P(None, ('gx', 'gy')), may hold values from -6 to 6
- incident: float32 [192, 65536], P(None, ('gx', 'gy')), may hold values from -6 to 6
- cost_grad: float32 [192, 65536], P(None, ('gx', 'gy')), may hold values from -6 to 6
- tmat_real: float32 [4, 96, 96], replicated, may hold values from -0.21875 to 0.21875
- tmat_imag: float32 [4, 96, 96], replicated, may hold values from -0.21875 to 0.21875
- translation_real: float32 [10, 96, 96], replicated, may hold values from -0.125 to 0.125
- translation_imaginary: float32 [10, 96, 96], replicated, may hold values from -0.125 to 0.125
- neighbours: int32 [10, 65536], P(None, ('gx', 'gy')), may hold values from -1 to 65535, as said below
- particle_type: int32 [65536], P(('gx', 'gy')), may hold values from 0 to 3
Outputs:
- adjoint: float32 [192, 65536], P(None, ('gx', 'gy'))
- sensitivity: float32 [4, 192, 192], replicated
Inputs may be any that keep to these rules, and one draw needn't show every extreme that they name: `neighbours`: particles sit on a lattice cut into spatial tiles of 4 rows (wide direction) by 32 columns (short direction); tile t holds slots t * 128 to t * 128 + 127, tiles numbered along the short direction fastest, and slot p of a tile sits at row p // 32 and column p % 32 of its tile. An entry of -1 marks an empty slot. Any other entry names a particle whose lattice row and column differ from the particle's own by dr and dc with 0 < dr^2 + dc^2 <= 5; the entries of one particle's list name distinct particles.
All inputs are finite; a program needn't handle non-finite values.
Results may differ from a plain program's by a relative error of at most 0.0001.
Values sent between devices are 32-bit elements; how exact they have to be, the bound alone decides.
No kernel may reach another device: no remote copies, remote signals or barrier semaphores. Data moves between devices by JAX's collectives and lax.ppermute only.
A program may use at most 64 MiB of HBM per device.

v0:
```python
import jax
import jax.numpy as jnp
from jax import lax
from jax.sharding import PartitionSpec as P

KRYLOV = 2
HIGH = lax.Precision.HIGHEST


def from_behind(block, axis, distance):
    devices = range(lax.axis_size(axis))
    route = [(i - distance, i) for i in devices if i - distance in devices]
    return lax.ppermute(block, axis, route)


def extended_2(x, sides, width):
    for axis, dim in sides:
        size, length = (lax.axis_size(axis), x.shape[dim])
        up = [(i, (i + 1) % size) for i in range(size - 1)]
        down = [(j, i) for i, j in up]
        last = lax.slice_in_dim(x, length - width, length, axis=dim)
        first = lax.slice_in_dim(x, 0, width, axis=dim)
        before = lax.ppermute(last, axis, up)
        after = lax.ppermute(first, axis, down)
        x = jnp.concatenate([before, x, after], axis=dim)
    return x


def complex_blocks(real_part, imag_part):
    upper_rows = jnp.concatenate([real_part, -imag_part], axis=2)
    lower_rows = jnp.concatenate([imag_part, real_part], axis=2)
    return jnp.concatenate([upper_rows, lower_rows], axis=1)


def small_solve(normal, right, steps):
    factor = jnp.linalg.cholesky(normal)
    forward_vals = []
    for row_index in range(steps):
        partial_sum = right[row_index]
        for col_index in range(row_index):
            partial_sum = partial_sum - factor[row_index, col_index] * forward_vals[col_index]
        forward_vals.append(partial_sum / factor[row_index, row_index])
    backward_vals = [None] * steps
    for row_index in reversed(range(steps)):
        partial_sum = forward_vals[row_index]
        for col_index in range(row_index + 1, steps):
            partial_sum = partial_sum - factor[col_index, row_index] * backward_vals[col_index]
        backward_vals[row_index] = partial_sum / factor[row_index, row_index]
    return backward_vals


def fold_wide(partial_value, dim):
    centre = jnp.take(partial_value, 1, axis=dim)
    for offset, piece in (
        (1, jnp.take(partial_value, 2, axis=dim)),
        (-1, jnp.take(partial_value, 0, axis=dim)),
    ):
        centre = centre + from_behind(piece, "gx", offset)
    return centre


def fold_short(partial_value, dim):
    centre = jnp.take(partial_value, 1, axis=dim)
    for offset, piece in (
        (1, jnp.take(partial_value, 2, axis=dim)),
        (-1, jnp.take(partial_value, 0, axis=dim)),
    ):
        centre = centre + from_behind(piece, "gy", offset)
    return centre


def body(
    forward_coeff,
    incident,
    cost_grad,
    tmat_real,
    tmat_imag,
    translation_real,
    translation_imaginary,
    neighbours,
    particle_type,
):
    width = forward_coeff.shape[0]
    local_count = forward_coeff.shape[1]
    kinds = tmat_real.shape[0]
    slots = translation_real.shape[0]
    steps = KRYLOV
    tmats = complex_blocks(tmat_real, tmat_imag)
    trans = complex_blocks(translation_real, translation_imaginary)
    tmat_stack = jnp.swapaxes(tmats, 1, 2).reshape(kinds * width, width)
    trans_adj = jnp.swapaxes(trans, 1, 2)
    kind_ids = jnp.arange(kinds, dtype=jnp.int32)
    type_mask = (particle_type[None, :] == kind_ids[:, None]).astype(jnp.float32)
    short_count = lax.axis_size("gy")
    tile = neighbours // local_count
    offset_x = tile // short_count - lax.axis_index("gx")
    offset_y = tile % short_count - lax.axis_index("gy")
    inner = neighbours % local_count
    target = (offset_x + 1) * (3 * local_count) + (offset_y + 1) * local_count + inner
    target = jnp.where(neighbours >= 0, target, 9 * local_count)
    flat_target = target.reshape(-1)
    extended = extended_2(
        forward_coeff.reshape(width, 1, 1, local_count), (("gx", 1), ("gy", 2)), 1
    )
    extended = jnp.concatenate(
        [extended.reshape(width, 9 * local_count), jnp.zeros((width, 1), jnp.float32)], axis=1
    )
    gathered = extended[:, target]
    exciting = incident + jnp.einsum("sdc,csp->dp", trans, gathered, precision=HIGH)
    beta = jnp.sqrt(lax.psum(jnp.sum(cost_grad * cost_grad), ("gx", "gy")))
    basis = [cost_grad / beta]
    columns = []
    for column in range(steps):
        vector = basis[column]
        all_kinds = jnp.dot(tmat_stack, vector, precision=HIGH).reshape(kinds, width, local_count)
        scaled = jnp.sum(type_mask[:, None, :] * all_kinds, axis=0)
        translated = jnp.einsum("sdc,cp->dsp", trans_adj, scaled, precision=HIGH).reshape(
            width, slots * local_count
        )
        collected = (
            jnp.zeros((width, 9 * local_count + 1), jnp.float32).at[:, flat_target].add(translated)
        )
        partial_value = collected[:, : 9 * local_count].reshape(width, 3, 3, local_count)
        summed = fold_short(fold_wide(partial_value, 1), 1)
        image = vector - summed
        local_dots = jnp.stack([jnp.sum(vec_item * image) for vec_item in basis])
        projections = lax.psum(local_dots, ("gx", "gy"))
        for row_index in range(column + 1):
            image = image - projections[row_index] * basis[row_index]
        height = jnp.sqrt(lax.psum(jnp.sum(image * image), ("gx", "gy")))
        columns.append(
            jnp.concatenate(
                [projections, height[None], jnp.zeros((steps - column - 1,), jnp.float32)]
            )
        )
        basis.append(image / height)
    hessen = jnp.stack(columns, axis=1)
    normal = jnp.dot(hessen.T, hessen, precision=HIGH)
    weights = small_solve(normal, beta * hessen[0], steps)
    adjoint = weights[0] * basis[0]
    column = 1
    adjoint = adjoint + weights[column] * basis[column]
    masked = adjoint[None, :, :] * type_mask[:, None, :]
    local_terms = jnp.einsum("kcp,dp->kcd", masked, exciting, precision=HIGH)
    sensitivity = lax.psum(local_terms, ("gx", "gy"))
    return (adjoint, sensitivity)


def solution(mesh):
    placed = (
        P(None, ("gx", "gy")),
        P(None, ("gx", "gy")),
        P(None, ("gx", "gy")),
        P(),
        P(),
        P(),
        P(),
        P(None, ("gx", "gy")),
        P(("gx", "gy")),
    )
    return jax.shard_map(
        body, mesh=mesh, in_specs=placed, out_specs=(P(None, ("gx", "gy")), P()), check_vma=False
    )
```

profile of v0, /device:TPU:23, one launch (start us, length us, event | category | flops | bytes accessed | tf_op | source)
XLA Modules:
  0.0 891.4 jit_solution(2647792898957183860)
XLA Ops:
  7.2 1.6 multiply_reduce_fusion.5
  8.8 102.0 %psum.42 = f32[]{:T(128)} all-reduce(f32[]{:T(128)} %multiply_reduce_fusion.5), channel_id=1, replica_groups=mesh['gx'=64,'gy'=8] {'gx','gy'}, use_global_device_ids=true, to_apply=%region_1.2 | all-reduce | flops 1 | bytes 8 | tf_op jit(solution)/shard_map/psum | solution.py:110
  114.8 1.8 fusion.10
  116.7 1.7 fusion.4
  119.2 8.3 scatter_custom_fusion
  127.9 4.7 collective-permute-start
  132.7 1.9 collective-permute-start.1
  134.8 3.9 collective-permute-done
  138.7 4.0 collective-permute-done.1
  142.8 1.4 collective-permute-start.2
  144.2 3.9 collective-permute-start.3
  149.8 100.7 %psum.43 = f32[1]{0:T(128)} all-reduce(f32[1]{0:T(128)} %bitcast.14), channel_id=1, replica_groups=mesh['gx'=64,'gy'=8] {'gx','gy'}, use_global_device_ids=true, to_apply=%region_5.12 | all-reduce | flops 1 | bytes 8 | tf_op jit(solution)/shard_map/psum | solution.py:127
  251.7 94.1 %psum.44 = f32[]{:T(128)} all-reduce(f32[]{:T(128)} %multiply_reduce_fusion.3), channel_id=1, replica_groups=mesh['gx'=64,'gy'=8] {'gx','gy'}, use_global_device_ids=true, to_apply=%region_7.14 | all-reduce | flops 1 | bytes 8 | tf_op jit(solution)/shard_map/psum | solution.py:130
  347.1 2.9 fusion.11
  350.0 1.7 fusion.7
  352.2 8.3 scatter_custom_fusion.1
  360.8 4.1 collective-permute-start.4
  365.8 1.9 collective-permute-start.5
  367.7 3.4 collective-permute-start.8
  371.1 1.9 collective-permute-start.9
  373.5 4.2 collective-permute-done.9
  379.0 4.4 collective-permute-start.11
  385.9 4.9 collective-permute-start.7
  391.4 4.1 gather_fusion
  395.5 1.6 multiply_reduce_fusion.2
  398.6 5.7 fusion.13
  404.3 98.6 %psum.45 = f32[2]{0:T(128)S(1)} all-reduce(f32[2]{0:T(128)S(1)} %pad_maximum_fusion.3), channel_id=1, replica_groups=mesh['gx'=64,'gy'=8] {'gx','gy'}, use_global_device_ids=true, to_apply=%region_12.19 | all-reduce | flops 2 | bytes 16 | tf_op jit(solution)/shard_map/psum | solution.py:127
  503.4 1.9 multiply_reduce_fusion
  506.1 94.3 %psum.46 = f32[]{:T(128)} all-reduce(f32[]{:T(128)} %multiply_reduce_fusion), channel_id=1, replica_groups=mesh['gx'=64,'gy'=8] {'gx','gy'}, use_global_device_ids=true, to_apply=%region_14.21 | all-reduce | flops 1 | bytes 8 | tf_op jit(solution)/shard_map/psum | solution.py:130
  609.3 1.7 fusion.18
  611.0 271.6 %all-reduce.3.cloned.1.call-done = f32[4,192,192]{2,1,0:T(8,128)} async-done(((f32[4,192,192]{2,1,0:T(8,128)}), f32[4,192,192]{2,1,0:T(8,128)}) %all-reduce.3.cloned.1.call-update) | async-done | bytes 589840 | tf_op jit(solution)/shard_map/psum | solution.py:145
  882.5 2.1 copy.46
  (98 shorter events, 20.3 us)
Async XLA Ops:
  7.2 107.4 %copy-start.1 = (f32[10,96,96]{2,1,0:T(8,128)S(1)}, f32[10,96,96]{2,1,0:T(8,128)}, u32[]{:S(2)}) copy-start(f32[10,96,96]{2,1,0:T(8,128)} %param.26) | copy-start | bytes 1105924
  7.2 875.4 %all-reduce.3.cloned.1.call-start = ((), (), s32[]{:S(2)}) async-start(), calls=%async_computation | async-start | bytes 1572864 | tf_op jit(solution)/shard_map/psum | solution.py:145
  112.2 234.9 %copy-start.14 = (f32[4,128]{1,0:T(4,128)}, f32[4,128]{1,0:T(4,128)S(1)}, u32[]{:S(2)}) copy-start(f32[4,128]{1,0:T(4,128)S(1)} %fusion.51) | copy-start | bytes 6148
  113.1 1.7 copy-start.12
  113.1 1.7 copy-start
  113.2 1.7 copy-start.10
  113.2 1.7 copy-start.17
  114.6 2.1 copy-start.2
  114.8 3.6 copy-start.5
  118.5 0.7 copy-start.16
  127.9 10.8 %collective-permute-start = (f32[192,3,128]{2,0,1:T(8,128)S(1)}, f32[192,3,128]{2,0,1:T(8,128)S(1)}, u32[]{:S(2)}, u32[]{:S(2)}) collective-permute-start(f32[192,3,128]{2,0,1:T(8,128)S(1)} %bitcast.131), channel_id=1, source_target_pairs={{0,8},{8,16},{16,24},{24,32},{32,40},{40,48},{48,56},{56,64},{64,7... | collective-permute-start | bytes 884744 | tf_op jit(solution)/shard_map/ppermute | solution.py:13
  132.7 9.9 %collective-permute-start.1 = (f32[192,3,128]{2,0,1:T(8,128)S(1)}, f32[192,3,128]{2,0,1:T(8,128)S(1)}, u32[]{:S(2)}, u32[]{:S(2)}) collective-permute-start(f32[192,3,128]{2,0,1:T(8,128)S(1)} %bitcast.132), channel_id=1, source_target_pairs={{8,0},{16,8},{24,16},{32,24},{40,32},{48,40},{56,48},{64,56},{72,6... | collective-permute-start | bytes 884744 | tf_op jit(solution)/shard_map/ppermute | solution.py:13
  134.8 212.3 %copy-start.11 = (f32[4,96,96]{2,1,0:T(8,128)S(1)}, f32[4,96,96]{2,1,0:T(8,128)}, u32[]{:S(2)}) copy-start(f32[4,96,96]{2,1,0:T(8,128)} %param.25) | copy-start | bytes 442372
  134.8 212.3 %copy-start.13 = (f32[4,96,96]{2,1,0:T(8,128)S(1)}, f32[4,96,96]{2,1,0:T(8,128)}, u32[]{:S(2)}) copy-start(f32[4,96,96]{2,1,0:T(8,128)} %copy-done.12) | copy-start | bytes 442372
  142.7 207.2 %copy-start.3 = (f32[10,96,96]{1,2,0:T(8,128)S(1)}, f32[10,96,96]{1,2,0:T(8,128)}, u32[]{:S(2)}) copy-start(f32[10,96,96]{1,2,0:T(8,128)} %copy-done.2) | copy-start | bytes 1105924
  142.7 207.2 %copy-start.6 = (f32[10,96,96]{1,2,0:T(8,128)S(1)}, f32[10,96,96]{1,2,0:T(8,128)}, u32[]{:S(2)}) copy-start(f32[10,96,96]{1,2,0:T(8,128)} %copy-done.5) | copy-start | bytes 1105924
  142.8 5.4 collective-permute-start.2
  144.2 4.8 collective-permute-start.3
  360.5 7.2 copy-start.8
  360.8 22.8 %collective-permute-start.4 = (f32[192,3,128]{2,0,1:T(8,128)S(1)}, f32[192,3,128]{2,0,1:T(8,128)S(1)}, u32[]{:S(2)}, u32[]{:S(2)}) collective-permute-start(f32[192,3,128]{2,0,1:T(8,128)S(1)} %bitcast.130), channel_id=1, source_target_pairs={{0,8},{8,16},{16,24},{24,32},{32,40},{40,48},{48,56},{56,64},{64,7... | collective-permute-start | bytes 884744 | tf_op jit(solution)/shard_map/ppermute | solution.py:13
  365.8 17.8 %collective-permute-start.5 = (f32[192,3,128]{2,0,1:T(8,128)}, f32[192,3,128]{2,0,1:T(8,128)}, u32[]{:S(2)}, u32[]{:S(2)}) collective-permute-start(f32[192,3,128]{2,0,1:T(8,128)} %bitcast.26), channel_id=1, source_target_pairs={{8,0},{16,8},{24,16},{32,24},{40,32},{48,40},{56,48},{64,56},{72,6... | collective-permute-start | bytes 884744 | tf_op jit(solution)/shard_map/ppermute | solution.py:13
  367.7 5.8 collective-permute-start.8
  371.1 6.6 collective-permute-start.9
  377.7 13.2 %collective-permute-start.10 = (f32[192,3,1,128]{3,0,2,1:T(8,128)S(1)}, f32[192,3,1,128]{3,0,2,1:T(8,128)S(1)}, u32[]{:S(2)}, u32[]{:S(2)}) collective-permute-start(f32[192,3,1,128]{3,0,2,1:T(8,128)S(1)} %pad_maximum_fusion.1), channel_id=1, source_target_pairs={{0,1},{1,2},{2,3},{3,4},{4,5},{5,6},{6,7},{8,9},{9,10},{10,11},{11... | collective-permute-start | bytes 884744 | tf_op jit(solution)/shard_map/ppermute | solution.py:23
  379.0 11.9 %collective-permute-start.11 = (f32[192,3,1,128]{3,0,2,1:T(8,128)S(1)}, f32[192,3,1,128]{3,0,2,1:T(8,128)S(1)}, u32[]{:S(2)}, u32[]{:S(2)}) collective-permute-start(f32[192,3,1,128]{3,0,2,1:T(8,128)S(1)} %pad_maximum_fusion.1), channel_id=1, source_target_pairs={{1,0},{2,1},{3,2},{4,3},{5,4},{6,5},{7,6},{9,8},{10,9},{11,10},{12... | collective-permute-start | bytes 884744 | tf_op jit(solution)/shard_map/ppermute | solution.py:24
  384.6 10.9 %collective-permute-start.6 = (f32[192,128]{1,0:T(8,128)S(1)}, f32[192,128]{1,0:T(8,128)}, u32[]{:S(2)}, u32[]{:S(2)}) collective-permute-start(f32[192,128]{1,0:T(8,128)S(1)} %get-tuple-element.87), channel_id=1, source_target_pairs={{0,1},{1,2},{2,3},{3,4},{4,5},{5,6},{6,7},{8,9},{9,10},{10,11},{11... | collective-permute-start | bytes 294920 | tf_op jit(solution)/shard_map/ppermute | solution.py:13
  385.9 9.6 %collective-permute-start.7 = (f32[192,128]{1,0:T(8,128)S(1)}, f32[192,128]{1,0:T(8,128)}, u32[]{:S(2)}, u32[]{:S(2)}) collective-permute-start(f32[192,128]{1,0:T(8,128)S(1)} %get-tuple-element.88), channel_id=1, source_target_pairs={{1,0},{2,1},{3,2},{4,3},{5,4},{6,5},{7,6},{9,8},{10,9},{11,10},{12... | collective-permute-start | bytes 294920 | tf_op jit(solution)/shard_map/ppermute | solution.py:13
  391.4 7.2 copy-start.4
  391.4 7.2 copy-start.7
  391.4 7.2 copy-start.18
  398.6 210.7 %copy-start.15 = (f32[4,128]{1,0:T(4,128)S(1)}, f32[4,128]{1,0:T(4,128)}, u32[]{:S(2)}) copy-start(f32[4,128]{1,0:T(4,128)} %copy-done.14) | copy-start | bytes 6148
  609.2 275.3 %copy-start.9 = (f32[192,128]{1,0:T(8,128)}, f32[192,128]{1,0:T(8,128)S(1)}, u32[]{:S(2)}) copy-start(f32[192,128]{1,0:T(8,128)S(1)} %multiply_add_fusion) | copy-start | bytes 294916
Sparse Core Ops, SparseCore 0:
  611.1 271.3 all-reduce.2
where the time goes:
time: 893 us; the launch traced here: 891 us
  blocking collectives  490 us (55%)
  waiting for transfers between devices  285 us (32%)
  starting transfers between devices  35.2 us (4%)
  other arithmetic  30.8 us (3%)
  between operations  21.8 us (2%)
  matrix products  15.7 us (2%)
  local copies, waits for them, and re-layouts  13.2 us (1%)
    psum x1, waiting for transfers between devices, body(): sensitivity = lax.psum(local_terms, ('gx', 'gy'))  272 us
    psum x2, blocking collectives, body(): projections = lax.psum(local_dots, ('gx', 'gy'))  199 us
    psum x2, blocking collectives, body(): height = jnp.sqrt(lax.psum(jnp.sum(image * image), ('gx', 'gy')))  188 us
    psum x1, blocking collectives, body(): beta = jnp.sqrt(lax.psum(jnp.sum(cost_grad * cost_grad), ('gx', 'gy')))  102 us
    ppermute x8, starting transfers between devices, from_behind(): return lax.ppermute(block, axis, route)  24.1 us
  transfers between devices with their start and end apart: 13, of which 6 were waited for; matrix products, arithmetic and copies ran while one was open for 1% of the time, Pallas kernels for 0%

commit v1 on v0

--- a/solution.py
+++ b/solution.py
@@ -124,7 +124,7 @@
         summed = fold_short(fold_wide(partial_value, 1), 1)
         image = vector - summed
         local_dots = jnp.stack([jnp.sum(vec_item * image) for vec_item in basis])
-        projections = lax.psum(local_dots, ("gx", "gy"))
+        projections = lax.psum(lax.psum(local_dots, "gy"), "gx")
         for row_index in range(column + 1):
             image = image - projections[row_index] * basis[row_index]
         height = jnp.sqrt(lax.psum(jnp.sum(image * image), ("gx", "gy")))

time: 893 us -> 1010 us (1.13)
  blocking collectives: 490 us -> 608 us
    psum x2, blocking collectives: 188 us -> 259 us  [body(): height = jnp.sqrt(lax.psum(jnp.sum(image * image), ('gx', 'gy')))]
    psum x2 -> x4, blocking collectives: 199 us -> 246 us  [body(): projections = lax.psum(lax.psum(local_dots, 'gy'), 'gx')]
  transfers between devices with their start and end apart: 13 -> 13, of which waited for: 6 -> 6; matrix products, arithmetic and copies ran while one was open for 1% -> 0% of each run, Pallas kernels for 0% -> 0%
where the time goes in v1:
time: 1010 us
  blocking collectives  608 us (60%)
  waiting for transfers between devices  286 us (28%)
  starting transfers between devices  35.1 us (3%)
  other arithmetic  31.3 us (3%)
  between operations  21.9 us (2%)
  matrix products  14.8 us (1%)
  local copies, waits for them, and re-layouts  12.3 us (1%)
    psum x1, waiting for transfers between devices, body(): sensitivity = lax.psum(local_terms, ('gx', 'gy'))  272 us
    psum x2, blocking collectives, body(): height = jnp.sqrt(lax.psum(jnp.sum(image * image), ('gx', 'gy')))  259 us
    psum x4, blocking collectives, body(): projections = lax.psum(lax.psum(local_dots, 'gy'), 'gx')  246 us
    psum x1, blocking collectives, body(): beta = jnp.sqrt(lax.psum(jnp.sum(cost_grad * cost_grad), ('gx', 'gy')))  102 us
    ppermute x8, starting transfers between devices, from_behind(): return lax.ppermute(block, axis, route)  24.5 us
  transfers between devices with their start and end apart: 13, of which 6 were waited for; matrix products, arithmetic and copies ran while one was open for 0% of the time, Pallas kernels for 0%

profile of v1, /device:TPU:23, one launch (start us, length us, event | category | flops | bytes accessed | tf_op | source)
XLA Modules:
  0.0 1009.1 jit_solution(16436459287751784827)
XLA Ops:
  8.8 102.0 %psum.56 = f32[]{:T(128)} all-reduce(f32[]{:T(128)} %multiply_reduce_fusion.5), channel_id=1, replica_groups=mesh['gx'=64,'gy'=8] {'gx','gy'}, use_global_device_ids=true, to_apply=%region_1.2 | all-reduce | flops 1 | bytes 8 | tf_op jit(solution)/shard_map/psum | solution.py:110
  114.8 1.8 fusion.10
  116.7 1.7 fusion.4
  119.2 8.3 scatter_custom_fusion
  127.9 4.7 collective-permute-start
  132.7 1.9 collective-permute-start.1
  134.8 3.9 collective-permute-done
  138.7 4.0 collective-permute-done.1
  144.2 3.9 collective-permute-start.3
  149.7 15.6 %psum.57 = f32[1]{0:T(128)} all-reduce(f32[1]{0:T(128)} %bitcast.14), channel_id=1, replica_groups=mesh['gx'=64,'gy'=8] {'gy'}, use_global_device_ids=true, to_apply=%region_5.12 | all-reduce | flops 1 | bytes 8 | tf_op jit(solution)/shard_map/psum | solution.py:127
  165.2 107.8 %psum.58 = f32[1]{0:T(128)} all-reduce(f32[1]{0:T(128)} %psum.57), channel_id=1, replica_groups=mesh['gx'=64,'gy'=8] {'gx'}, use_global_device_ids=true, to_apply=%region_6.13 | all-reduce | flops 1 | bytes 8 | tf_op jit(solution)/shard_map/psum | solution.py:127
  274.3 126.4 %psum.59 = f32[]{:T(128)} all-reduce(f32[]{:T(128)} %multiply_reduce_fusion.3), channel_id=1, replica_groups=mesh['gx'=64,'gy'=8] {'gx','gy'}, use_global_device_ids=true, to_apply=%region_8.15 | all-reduce | flops 1 | bytes 8 | tf_op jit(solution)/shard_map/psum | solution.py:130
  402.1 1.8 fusion.11
  404.0 1.7 fusion.7
  406.1 8.3 scatter_custom_fusion.1
  414.8 4.3 collective-permute-start.4
  420.0 2.1 collective-permute-start.5
  422.1 3.2 collective-permute-start.8
  425.3 2.1 collective-permute-start.9
  428.0 4.2 collective-permute-done.9
  433.6 3.9 collective-permute-start.11
  440.0 4.9 collective-permute-start.7
  445.5 2.2 multiply_reduce_fusion.2
  449.0 3.1 gather_fusion
  452.2 15.0 %psum.60 = f32[2]{0:T(128)S(1)} all-reduce(f32[2]{0:T(128)S(1)} %pad_maximum_fusion.3), channel_id=1, replica_groups=mesh['gx'=64,'gy'=8] {'gy'}, use_global_device_ids=true, to_apply=%region_13.20 | all-reduce | flops 2 | bytes 16 | tf_op jit(solution)/shard_map/psum | solution.py:127
  467.2 5.8 fusion.13
  473.0 108.1 %psum.61 = f32[2]{0:T(128)S(1)} all-reduce(f32[2]{0:T(128)S(1)} %psum.60), channel_id=1, replica_groups=mesh['gx'=64,'gy'=8] {'gx'}, use_global_device_ids=true, to_apply=%region_14.21 | all-reduce | flops 2 | bytes 16 | tf_op jit(solution)/shard_map/psum | solution.py:127
  581.7 2.0 multiply_reduce_fusion
  584.4 133.1 %psum.62 = f32[]{:T(128)} all-reduce(f32[]{:T(128)} %multiply_reduce_fusion), channel_id=1, replica_groups=mesh['gx'=64,'gy'=8] {'gx','gy'}, use_global_device_ids=true, to_apply=%region_16.23 | all-reduce | flops 1 | bytes 8 | tf_op jit(solution)/shard_map/psum | solution.py:130
  726.4 1.7 fusion.18
  728.1 272.1 %all-reduce.3.cloned.1.call-done = f32[4,192,192]{2,1,0:T(8,128)} async-done(((f32[4,192,192]{2,1,0:T(8,128)}), f32[4,192,192]{2,1,0:T(8,128)}) %all-reduce.3.cloned.1.call-update) | async-done | bytes 589840 | tf_op jit(solution)/shard_map/psum | solution.py:145
  1000.2 2.1 copy.46
  (98 shorter events, 23.3 us)
Async XLA Ops:
  7.2 107.4 %copy-start.1 = (f32[10,96,96]{2,1,0:T(8,128)S(1)}, f32[10,96,96]{2,1,0:T(8,128)}, u32[]{:S(2)}) copy-start(f32[10,96,96]{2,1,0:T(8,128)} %param.26) | copy-start | bytes 1105924
  7.2 993.0 %all-reduce.3.cloned.1.call-start = ((), (), s32[]{:S(2)}) async-start(), calls=%async_computation | async-start | bytes 1572864 | tf_op jit(solution)/shard_map/psum | solution.py:145
  112.2 289.9 %copy-start.13 = (f32[4,128]{1,0:T(4,128)}, f32[4,128]{1,0:T(4,128)S(1)}, u32[]{:S(2)}) copy-start(f32[4,128]{1,0:T(4,128)S(1)} %fusion.51) | copy-start | bytes 6148
  113.1 1.7 copy-start.11
  113.1 1.7 copy-start
  113.1 1.7 copy-start.9
  113.2 1.7 copy-start.16
  114.6 2.1 copy-start.2
  114.8 3.6 copy-start.4
  118.4 0.7 copy-start.15
  127.9 10.8 %collective-permute-start = (f32[192,3,128]{2,0,1:T(8,128)S(1)}, f32[192,3,128]{2,0,1:T(8,128)S(1)}, u32[]{:S(2)}, u32[]{:S(2)}) collective-permute-start(f32[192,3,128]{2,0,1:T(8,128)S(1)} %bitcast.131), channel_id=1, source_target_pairs={{0,8},{8,16},{16,24},{24,32},{32,40},{40,48},{48,56},{56,64},{64,7... | collective-permute-start | bytes 884744 | tf_op jit(solution)/shard_map/ppermute | solution.py:13
  132.7 9.9 collective-permute-start.1
  134.8 267.3 %copy-start.10 = (f32[4,96,96]{2,1,0:T(8,128)S(1)}, f32[4,96,96]{2,1,0:T(8,128)}, u32[]{:S(2)}) copy-start(f32[4,96,96]{2,1,0:T(8,128)} %param.25) | copy-start | bytes 442372
  134.8 267.3 %copy-start.12 = (f32[4,96,96]{2,1,0:T(8,128)S(1)}, f32[4,96,96]{2,1,0:T(8,128)}, u32[]{:S(2)}) copy-start(f32[4,96,96]{2,1,0:T(8,128)} %copy-done.11) | copy-start | bytes 442372
  134.8 267.3 %copy-start.17 = (f32[4,96,96]{2,1,0:T(8,128)S(1)}, f32[4,96,96]{2,1,0:T(8,128)}, u32[]{:S(2)}) copy-start(f32[4,96,96]{2,1,0:T(8,128)} %param.24) | copy-start | bytes 442372
  142.7 261.2 %copy-start.3 = (f32[10,96,96]{1,2,0:T(8,128)S(1)}, f32[10,96,96]{1,2,0:T(8,128)}, u32[]{:S(2)}) copy-start(f32[10,96,96]{1,2,0:T(8,128)} %copy-done.2) | copy-start | bytes 1105924
  142.7 261.2 %copy-start.5 = (f32[10,96,96]{1,2,0:T(8,128)S(1)}, f32[10,96,96]{1,2,0:T(8,128)}, u32[]{:S(2)}) copy-start(f32[10,96,96]{1,2,0:T(8,128)} %copy-done.4) | copy-start | bytes 1105924
  142.8 5.4 collective-permute-start.2
  144.2 4.8 collective-permute-start.3
  414.5 7.6 copy-start.6
  414.8 22.9 %collective-permute-start.4 = (f32[192,3,128]{2,0,1:T(8,128)S(1)}, f32[192,3,128]{2,0,1:T(8,128)S(1)}, u32[]{:S(2)}, u32[]{:S(2)}) collective-permute-start(f32[192,3,128]{2,0,1:T(8,128)S(1)} %bitcast.130), channel_id=1, source_target_pairs={{0,8},{8,16},{16,24},{24,32},{32,40},{40,48},{48,56},{56,64},{64,7... | collective-permute-start | bytes 884744 | tf_op jit(solution)/shard_map/ppermute | solution.py:13
  420.0 17.7 %collective-permute-start.5 = (f32[192,3,128]{2,0,1:T(8,128)}, f32[192,3,128]{2,0,1:T(8,128)}, u32[]{:S(2)}, u32[]{:S(2)}) collective-permute-start(f32[192,3,128]{2,0,1:T(8,128)} %bitcast.26), channel_id=1, source_target_pairs={{8,0},{16,8},{24,16},{32,24},{40,32},{48,40},{56,48},{64,56},{72,6... | collective-permute-start | bytes 884744 | tf_op jit(solution)/shard_map/ppermute | solution.py:13
  422.1 5.9 collective-permute-start.8
  425.3 6.9 collective-permute-start.9
  432.3 12.6 %collective-permute-start.10 = (f32[192,3,1,128]{3,0,2,1:T(8,128)S(1)}, f32[192,3,1,128]{3,0,2,1:T(8,128)S(1)}, u32[]{:S(2)}, u32[]{:S(2)}) collective-permute-start(f32[192,3,1,128]{3,0,2,1:T(8,128)S(1)} %pad_maximum_fusion.1), channel_id=1, source_target_pairs={{0,1},{1,2},{2,3},{3,4},{4,5},{5,6},{6,7},{8,9},{9,10},{10,11},{11... | collective-permute-start | bytes 884744 | tf_op jit(solution)/shard_map/ppermute | solution.py:23
  433.6 11.3 %collective-permute-start.11 = (f32[192,3,1,128]{3,0,2,1:T(8,128)S(1)}, f32[192,3,1,128]{3,0,2,1:T(8,128)S(1)}, u32[]{:S(2)}, u32[]{:S(2)}) collective-permute-start(f32[192,3,1,128]{3,0,2,1:T(8,128)S(1)} %pad_maximum_fusion.1), channel_id=1, source_target_pairs={{1,0},{2,1},{3,2},{4,3},{5,4},{6,5},{7,6},{9,8},{10,9},{11,10},{12... | collective-permute-start | bytes 884744 | tf_op jit(solution)/shard_map/ppermute | solution.py:24
  438.7 6.7 collective-permute-start.6
  440.0 5.4 collective-permute-start.7
  467.2 114.5 %copy-start.7 = (f32[192,128]{1,0:T(8,128)S(1)}, f32[192,128]{1,0:T(8,128)}, u32[]{:S(2)}) copy-start(f32[192,128]{1,0:T(8,128)} %get-tuple-element.78) | copy-start | bytes 294916
  467.2 259.2 %copy-start.14 = (f32[4,128]{1,0:T(4,128)S(1)}, f32[4,128]{1,0:T(4,128)}, u32[]{:S(2)}) copy-start(f32[4,128]{1,0:T(4,128)} %copy-done.13) | copy-start | bytes 6148
  726.4 275.9 %copy-start.8 = (f32[192,128]{1,0:T(8,128)}, f32[192,128]{1,0:T(8,128)S(1)}, u32[]{:S(2)}) copy-start(f32[192,128]{1,0:T(8,128)S(1)} %multiply_add_fusion) | copy-start | bytes 294916
Sparse Core Ops, SparseCore 0:
  728.2 271.8 all-reduce.2
